TPU v7x, 256 devices: a whole 4x4x8 slice. The times are simulated.
256 devices in a mesh: batch: 16 (over y, x), proto: 16 (over z, core).
Axes of the slice: x: 4, y: 4, z: 8, core: 2. Of those that a mesh axis runs over, the one named last changes fastest.
Arguments:
- teacher_emb: bfloat16 [256, 8192], P('proto', 'batch'), may hold values from -22 to 22
- student_emb: bfloat16 [256, 8192], P('proto', 'batch'), may hold values from -6 to 6
- prototypes: bfloat16 [256, 65536], P('batch', 'proto'), may hold values from -16 to 16
Outputs:
- grad_proto: float32 [256, 65536], P('batch', 'proto')
- grad_student: float32 [256, 8192], P('proto', 'batch')
- loss: float32 [], replicated
All inputs are finite; a program needn't handle non-finite values.
Results may differ from a plain program's by a relative error of at most 0.00055.
The roundings to bfloat16 on the way count: a program that leaves them out, or rounds other values in their place, can miss the bound.
Values may be sent and summed in bfloat16 or wider, within the bound.
A program may use at most 64 MiB of HBM per device.

v0:
```python
import jax
import jax.numpy as jnp
from jax import lax
from jax.sharding import PartitionSpec as P

ITERS = 3
teacher_temp = 0.07
student_temp = 0.1
epsilon = 1e-06


def unit(matrix):
    values = matrix.astype(jnp.float32)
    factor = lax.rsqrt(jnp.sum(values * values, axis=0, keepdims=True) + epsilon)
    return ((values * factor).astype(jnp.bfloat16), factor)


def cosine(left, right):
    return lax.dot_general(
        left, right, (((0,), (0,)), ((), ())), preferred_element_type=jnp.float32
    )


def shards(teacher_emb, student_emb, prototypes):
    teacher_full, student_full = (
        lax.all_gather(teacher_emb, "proto", axis=0, tiled=True),
        lax.all_gather(student_emb, "proto", axis=0, tiled=True),
    )
    proto_full = lax.all_gather(prototypes, "batch", axis=0, tiled=True)
    proto_unit, proto_scale = unit(proto_full)
    teacher_unit, unused = unit(teacher_full)
    student_unit, student_scale = unit(student_full)
    width = proto_full.shape[0]
    local_rows = teacher_full.shape[1]
    total_rows = local_rows * lax.axis_size("batch")
    expo = jnp.exp(cosine(teacher_unit, proto_unit) / teacher_temp)
    targets = expo
    for iteration in range(ITERS):
        column_total = lax.psum(jnp.sum(targets, axis=0), "batch")
        targets = targets / column_total[None, :]
        row_total = lax.psum(jnp.sum(targets, axis=1), "proto")
        targets = targets / row_total[:, None]
    cos_student = cosine(student_unit, proto_unit)
    logits = cos_student / student_temp
    partial_total = jnp.sum(jnp.exp(logits), axis=1)
    softmax_total = lax.psum(partial_total, "proto")
    logp = logits - jnp.log(softmax_total)[:, None]
    loss_part = -jnp.sum(targets * logp)
    loss = lax.psum(loss_part, ("batch", "proto")) / total_rows
    grad_logit = ((jnp.exp(logp) - targets) / (total_rows * student_temp)).astype(jnp.bfloat16)
    proto_rows = width // lax.axis_size("batch")
    crop_rows = width // lax.axis_size("proto")
    proto_start = lax.axis_index("batch") * proto_rows
    crop_start = lax.axis_index("proto") * crop_rows
    proto_own = lax.dynamic_slice_in_dim(proto_unit, proto_start, proto_rows, 0).astype(jnp.float32)
    student_own = lax.dynamic_slice_in_dim(student_unit, crop_start, crop_rows, 0).astype(
        jnp.float32
    )
    rows = student_unit
    whole_grad = lax.psum(jnp.dot(rows, grad_logit, preferred_element_type=jnp.float32), "batch")
    proto_part = lax.dynamic_slice_in_dim(whole_grad, proto_start, proto_rows, 0)
    rows = proto_unit
    crop_part = lax.psum_scatter(
        lax.dot_general(
            rows, grad_logit, (((1,), (1,)), ((), ())), preferred_element_type=jnp.float32
        ),
        "proto",
        scatter_dimension=0,
        tiled=True,
    )
    proto_dot = lax.psum(jnp.sum(proto_own * proto_part, axis=0), "batch")
    crop_dot = lax.psum(jnp.sum(student_own * crop_part, axis=0), "proto")
    grad_proto = (proto_part - proto_own * proto_dot[None, :]) * proto_scale
    grad_student = (crop_part - student_own * crop_dot[None, :]) * student_scale
    return (grad_proto, grad_student, loss)


def solution(mesh):
    in_specs = (P("proto", "batch"), P("proto", "batch"), P("batch", "proto"))
    out_specs = (P("batch", "proto"), P("proto", "batch"), P())
    return jax.shard_map(shards, mesh=mesh, in_specs=in_specs, out_specs=out_specs, check_vma=False)
```

profile of v0, /device:TPU:32, one launch (start us, length us, event | category | flops | bytes accessed | tf_op | source)
XLA Modules:
  0.0 646.7 jit_solution(15893222598696431938)
XLA Ops:
  7.2 0.7 all-gather.2.cloned.1.call-update
  7.9 18.8 %all_gather.11 = bf16[256,512]{1,0:T(8,128)(2,1)S(1)} all-gather(bf16[16,512]{1,0:T(8,128)(2,1)} %param.3), channel_id=1, replica_groups=mesh['batch'=16,'proto'=16] {'proto'}, dimensions={0}, use_global_device_ids=true | all-gather | bytes 278528 | tf_op jit(solution)/shard_map/all_gather | solution.py:26
  26.7 17.3 %all_gather.9 = bf16[256,512]{1,0:T(8,128)(2,1)S(1)} all-gather(bf16[16,512]{1,0:T(8,128)(2,1)} %param.4), channel_id=1, replica_groups=mesh['batch'=16,'proto'=16] {'proto'}, dimensions={0}, use_global_device_ids=true | all-gather | bytes 278528 | tf_op jit(solution)/shard_map/all_gather | solution.py:27
  44.0 0.1 fusion.15
  44.2 18.8 %all-gather.2.cloned.1.call-done = bf16[256,4096]{1,0:T(8,128)(2,1)} async-done(((bf16[16,4096]{1,0:T(8,128)(2,1)}), bf16[256,4096]{1,0:T(8,128)(2,1)}) %all-gather.2.cloned.1.call-update) | async-done | bytes 2097168 | tf_op jit(solution)/shard_map/all_gather | solution.py:29
  63.0 2.0 fusion.11
  65.1 2.1 fusion.12
  67.1 4.7 fusion.25
  71.8 72.1 %psum.78 = f32[4096]{0:T(1024)S(1)} all-reduce(f32[4096]{0:T(1024)S(1)} %get-tuple-element.9), channel_id=1, replica_groups=mesh['batch'=16,'proto'=16] {'batch'}, use_global_device_ids=true, to_apply=%region_6.0 | all-reduce | flops 4096 | bytes 32768 | tf_op jit(solution)/shard_map/psum | solution.py:39
  143.9 4.0 divide_reduce_fusion
  147.9 20.5 %psum.79 = f32[512]{0:T(512)S(1)} all-reduce(f32[512]{0:T(512)S(1)} %divide_reduce_fusion), channel_id=1, replica_groups=mesh['batch'=16,'proto'=16] {'proto'}, use_global_device_ids=true, to_apply=%region_8.0 | all-reduce | flops 512 | bytes 4096 | tf_op jit(solution)/shard_map/psum | solution.py:41
  168.4 4.7 fusion.7
  173.2 69.5 %psum.80 = f32[4096]{0:T(1024)S(1)} all-reduce(f32[4096]{0:T(1024)S(1)} %fusion.7), channel_id=1, replica_groups=mesh['batch'=16,'proto'=16] {'batch'}, use_global_device_ids=true, to_apply=%region_10.0 | all-reduce | flops 4096 | bytes 32768 | tf_op jit(solution)/shard_map/psum | solution.py:39
  242.7 4.3 fusion.8
  247.0 23.5 %psum.81 = f32[512]{0:T(512)S(1)} all-reduce(f32[512]{0:T(512)S(1)} %fusion.8), channel_id=1, replica_groups=mesh['batch'=16,'proto'=16] {'proto'}, use_global_device_ids=true, to_apply=%region_12.0 | all-reduce | flops 512 | bytes 4096 | tf_op jit(solution)/shard_map/psum | solution.py:41
  270.6 4.5 fusion.9
  275.0 69.5 %psum.82 = f32[4096]{0:T(1024)S(1)} all-reduce(f32[4096]{0:T(1024)S(1)} %fusion.9), channel_id=1, replica_groups=mesh['batch'=16,'proto'=16] {'batch'}, use_global_device_ids=true, to_apply=%region_14.0 | all-reduce | flops 4096 | bytes 32768 | tf_op jit(solution)/shard_map/psum | solution.py:39
  344.6 4.6 fusion.10
  349.2 4.6 exponential_reduce_fusion
  353.8 23.7 %all-reduce = (f32[512]{0:T(512)S(1)}, f32[512]{0:T(512)S(1)}) all-reduce(f32[512]{0:T(512)S(1)} %get-tuple-element.7, f32[512]{0:T(512)S(1)} %fusion.10), channel_id=1, replica_groups=mesh['batch'=16,'proto'=16] {'proto'}, use_global_device_ids=true, to_apply=%region_3.0 | all-reduce | flops 1024 | bytes 8192 | tf_op jit(solution)/shard_map/psum | solution.py:46
  377.5 9.5 %multiply_reduce_fusion = (f32[]{:T(128)}, bf16[512,4096]{1,0:T(8,128)(2,1)S(1)}) fusion(f32[512,4096]{1,0:T(8,128)} %get-tuple-element.8, f32[512]{0:T(512)S(1)} %log.3, f32[512,4096]{1,0:T(8,128)} %get-tuple-element.10, f32[512]{0:T(512)S(1)} %get-tuple-element.4, f32[4096]{0:T(1024)S(1)} %psum.82, f32[512]{0:T(512)S(1)} %psum.81, f32[4096]{0:T(1024)S(1)} %psum.80, ...), kind=kLoop, calls=%fused_computation.9 | loop fusion | flops 27262976 | bytes 21028868 | tf_op jit(solution)/shard_map/reduce_sum | solution.py:48
  387.0 2.0 copy-done
  389.0 2.1 fusion.27
  391.2 5.4 fusion.26
  397.2 78.2 %psum.87 = f32[]{:T(128)} all-reduce(f32[]{:T(128)S(6)} %neg.3), channel_id=1, replica_groups=mesh['batch'=16,'proto'=16] {'batch','proto'}, use_global_device_ids=true, to_apply=%region_24.0 | all-reduce | flops 1 | bytes 8 | tf_op jit(solution)/shard_map/psum | solution.py:49
  476.2 0.8 fusion.22
  476.9 22.5 %psum.86 = f32[512]{0:T(512)S(1)} all-reduce(f32[512]{0:T(512)S(1)} %fusion.22), channel_id=1, replica_groups=mesh['batch'=16,'proto'=16] {'proto'}, use_global_device_ids=true, to_apply=%region_22.0 | all-reduce | flops 512 | bytes 4096 | tf_op jit(solution)/shard_map/psum | solution.py:72
  499.4 1.4 fusion.24
  500.8 63.2 %all-reduce.3.cloned.1.call-done = f32[256,4096]{1,0:T(8,128)} async-done(((f32[256,4096]{1,0:T(8,128)}), f32[256,4096]{1,0:T(8,128)}) %all-reduce.3.cloned.1.call-update) | async-done | bytes 4194320 | tf_op jit(solution)/shard_map/psum | solution.py:60
  564.0 1.0 fusion.17
  565.0 72.4 %psum.85 = f32[4096]{0:T(1024)S(1)} all-reduce(f32[4096]{0:T(1024)S(1)} %fusion.17), channel_id=1, replica_groups=mesh['batch'=16,'proto'=16] {'batch'}, use_global_device_ids=true, to_apply=%region_19.0 | all-reduce | flops 4096 | bytes 32768 | tf_op jit(solution)/shard_map/psum | solution.py:71
  637.4 1.7 fusion.19
  (13 shorter events, 0.3 us)
Async XLA Ops:
  7.2 55.8 %all-gather.2.cloned.1.call-start = ((), (), s32[]{:S(2)}) async-start(), calls=%async_computation.1 | async-start | bytes 2228224 | tf_op jit(solution)/shard_map/all_gather | solution.py:29
  7.9 468.3 %reduce-scatter.2.cloned.1.call-start = ((), (), s32[]{:S(2)}) async-start(), calls=%async_computation.3 | async-start | bytes 557056 | tf_op jit(solution)/shard_map/reduce_scatter | solution.py:63
  387.0 2.0 copy-start
  391.1 172.9 %all-reduce.3.cloned.1.call-start = ((), (), s32[]{:S(2)}) async-start(), calls=%async_computation.2 | async-start | bytes 8388608 | tf_op jit(solution)/shard_map/psum | solution.py:60
Sparse Core Ops, SparseCore 0:
  10.4 52.5 all-gather.1
  391.3 53.1 reduce-scatter.1
  448.2 115.7 all-reduce.2
where the time goes:
time: 647 us
  blocking collectives  488 us (75%)
  waiting for transfers between devices  82.7 us (13%)
  other arithmetic  40.8 us (6%)
  matrix products  16.9 us (3%)
  between operations  16.2 us (3%)
    psum x3, blocking collectives, shards(): column_total = lax.psum(jnp.sum(targets, axis=0), 'batch')  211 us
    psum x1, blocking collectives, shards(): loss = lax.psum(loss_part, ('batch', 'proto')) / total_rows  78.2 us
    psum x1, blocking collectives, shards(): proto_dot = lax.psum(jnp.sum(proto_own * proto_part, axis=0), 'batch')  72.4 us
    psum x1, waiting for transfers between devices, shards(): lax.psum(jnp.dot(rows, grad_logit, preferred_element_type=jnp.float32), '...  63.2 us
    psum x2, blocking collectives, shards(): row_total = lax.psum(jnp.sum(targets, axis=1), 'proto')  44.1 us
    psum x1, blocking collectives, shards(): softmax_total = lax.psum(partial_total, 'proto')  23.7 us
    psum x1, blocking collectives, shards(): crop_dot = lax.psum(jnp.sum(student_own * crop_part, axis=0), 'proto')  22.5 us
    all_gather x1, blocking collectives, shards(): lax.all_gather(teacher_emb, 'proto', axis=0, tiled=True)  18.8 us
  transfers between devices with their start and end apart: 3, of which 2 were waited for; matrix products, arithmetic and copies ran while one was open for 1% of the time, Pallas kernels for 0%

commit v1 on v0

--- a/solution.py
+++ b/solution.py
@@ -7,6 +7,27 @@
 teacher_temp = 0.07
 student_temp = 0.1
 epsilon = 1e-06
+
+
+def ring_gather(array, axis, dim):
+    peers, index, extent = (lax.axis_size(axis), lax.axis_index(axis), array.shape[dim])
+    right = [(i, (i + 1) % peers) for i in range(peers)]
+    left = [(i, (i - 1) % peers) for i in range(peers)]
+    whole = jnp.zeros((*array.shape[:dim], peers * extent, *array.shape[dim + 1 :]), array.dtype)
+    whole = lax.dynamic_update_slice_in_dim(whole, array, index * extent, axis=dim)
+    from_left = from_right = array
+    half = peers // 2
+    for step in range(1, half + 1):
+        from_left = lax.ppermute(from_left, axis, right)
+        whole = lax.dynamic_update_slice_in_dim(
+            whole, from_left, (index - step) % peers * extent, axis=dim
+        )
+        if step < peers - half:
+            from_right = lax.ppermute(from_right, axis, left)
+            whole = lax.dynamic_update_slice_in_dim(
+                whole, from_right, (index + step) % peers * extent, axis=dim
+            )
+    return whole
 
 
 def unit(matrix):
@@ -23,7 +44,7 @@
 
 def shards(teacher_emb, student_emb, prototypes):
     teacher_full, student_full = (
-        lax.all_gather(teacher_emb, "proto", axis=0, tiled=True),
+        ring_gather(teacher_emb, "proto", 0),
         lax.all_gather(student_emb, "proto", axis=0, tiled=True),
     )
     proto_full = lax.all_gather(prototypes, "batch", axis=0, tiled=True)

time: 647 us -> 648 us (level)
  blocking collectives: 488 us -> 472 us
  starting transfers between devices: 0.12 us -> 11.3 us
    all_gather x1 -> x0, blocking collectives: 18.8 us -> none  [shards(): lax.all_gather(teacher_emb, 'proto', axis=0, tiled=True)]
    ppermute x0 -> x15, waiting for transfers between devices: none -> 15.3 us  [the longest x8 8.18 us: ring_gather(): from_left = lax.ppermute(from_left, axis, right)]
    all_gather x1, waiting for transfers between devices: 18.8 us -> 7.44 us  [shards(): proto_full = lax.all_gather(prototypes, 'batch', axis=0, tiled=True)]
    ppermute x0 -> x15, starting transfers between devices: none -> 11.2 us  [the longest x7 10.7 us: ring_gather(): from_right = lax.ppermute(from_right, axis, left)]
  transfers between devices with their start and end apart: 3 -> 18, of which waited for: 2 -> 10; matrix products, arithmetic and copies ran while one was open for 1% -> 1% of each run, Pallas kernels for 0% -> 0%
where the time goes in v1:
time: 648 us; the launch traced here: 647 us
  blocking collectives  472 us (73%)
  waiting for transfers between devices  86.7 us (13%)
  other arithmetic  40.8 us (6%)
  matrix products  16.8 us (3%)
  between operations  16.3 us (3%)
  starting transfers between devices  11.3 us (2%)
    psum x3, blocking collectives, shards(): column_total = lax.psum(jnp.sum(targets, axis=0), 'batch')  211 us
    psum x1, blocking collectives, shards(): loss = lax.psum(loss_part, ('batch', 'proto')) / total_rows  77.3 us
    psum x1, blocking collectives, shards(): proto_dot = lax.psum(jnp.sum(proto_own * proto_part, axis=0), 'batch')  72.4 us
    psum x1, waiting for transfers between devices, shards(): lax.psum(jnp.dot(rows, grad_logit, preferred_element_type=jnp.float32), '...  63.2 us
    psum x2, blocking collectives, shards(): row_total = lax.psum(jnp.sum(targets, axis=1), 'proto')  46 us
    psum x1, blocking collectives, shards(): softmax_total = lax.psum(partial_total, 'proto')  23.7 us
    psum x1, blocking collectives, shards(): crop_dot = lax.psum(jnp.sum(student_own * crop_part, axis=0), 'proto')  21.5 us
    all_gather x1, blocking collectives, shards(): lax.all_gather(student_emb, 'proto', axis=0, tiled=True)  20 us
  transfers between devices with their start and end apart: 18, of which 10 were waited for; matrix products, arithmetic and copies ran while one was open for 1% of the time, Pallas kernels for 0%

profile of v1, /device:TPU:32, one launch (start us, length us, event | category | flops | bytes accessed | tf_op | source)
XLA Modules:
  0.0 646.8 jit_solution(1465383283612602377)
XLA Ops:
  8.5 20.0 %all_gather.6 = bf16[256,512]{1,0:T(8,128)(2,1)S(1)} all-gather(bf16[16,512]{1,0:T(8,128)(2,1)} %param.4), channel_id=1, replica_groups=mesh['batch'=16,'proto'=16] {'proto'}, dimensions={0}, use_global_device_ids=true | all-gather | bytes 278528 | tf_op jit(solution)/shard_map/all_gather | solution.py:48
  31.8 2.1 collective-permute-start.5
  35.4 2.1 collective-permute-start.7
  38.9 1.7 collective-permute-start.9
  42.1 2.0 collective-permute-start.11
  45.5 1.7 collective-permute-start.13
  47.5 4.4 collective-permute-done.12
  51.9 3.6 collective-permute-done.14
  55.6 7.4 %all-gather.2.cloned.1.call-done = bf16[256,4096]{1,0:T(8,128)(2,1)} async-done(((bf16[16,4096]{1,0:T(8,128)(2,1)}), bf16[256,4096]{1,0:T(8,128)(2,1)}) %all-gather.2.cloned.1.call-update) | async-done | bytes 2097168 | tf_op jit(solution)/shard_map/all_gather | solution.py:50
  63.0 2.0 fusion.11
  65.1 2.1 fusion.12
  67.1 4.7 fusion.25
  71.8 72.1 %psum.78 = f32[4096]{0:T(1024)S(1)} all-reduce(f32[4096]{0:T(1024)S(1)} %get-tuple-element.9), channel_id=1, replica_groups=mesh['batch'=16,'proto'=16] {'batch'}, use_global_device_ids=true, to_apply=%region_6.7 | all-reduce | flops 4096 | bytes 32768 | tf_op jit(solution)/shard_map/psum | solution.py:60
  143.9 4.0 divide_reduce_fusion
  147.9 22.5 %psum.79 = f32[512]{0:T(512)S(1)} all-reduce(f32[512]{0:T(512)S(1)} %divide_reduce_fusion), channel_id=1, replica_groups=mesh['batch'=16,'proto'=16] {'proto'}, use_global_device_ids=true, to_apply=%region_8.9 | all-reduce | flops 512 | bytes 4096 | tf_op jit(solution)/shard_map/psum | solution.py:62
  170.4 4.7 fusion.7
  175.1 69.5 %psum.80 = f32[4096]{0:T(1024)S(1)} all-reduce(f32[4096]{0:T(1024)S(1)} %fusion.7), channel_id=1, replica_groups=mesh['batch'=16,'proto'=16] {'batch'}, use_global_device_ids=true, to_apply=%region_10.11 | all-reduce | flops 4096 | bytes 32768 | tf_op jit(solution)/shard_map/psum | solution.py:60
  244.6 4.3 fusion.8
  249.0 23.5 %psum.81 = f32[512]{0:T(512)S(1)} all-reduce(f32[512]{0:T(512)S(1)} %fusion.8), channel_id=1, replica_groups=mesh['batch'=16,'proto'=16] {'proto'}, use_global_device_ids=true, to_apply=%region_12.13 | all-reduce | flops 512 | bytes 4096 | tf_op jit(solution)/shard_map/psum | solution.py:62
  272.5 4.5 fusion.9
  277.0 69.5 %psum.82 = f32[4096]{0:T(1024)S(1)} all-reduce(f32[4096]{0:T(1024)S(1)} %fusion.9), channel_id=1, replica_groups=mesh['batch'=16,'proto'=16] {'batch'}, use_global_device_ids=true, to_apply=%region_14.15 | all-reduce | flops 4096 | bytes 32768 | tf_op jit(solution)/shard_map/psum | solution.py:60
  346.5 4.6 fusion.10
  351.1 4.6 exponential_reduce_fusion
  355.7 23.7 %all-reduce = (f32[512]{0:T(512)S(1)}, f32[512]{0:T(512)S(1)}) all-reduce(f32[512]{0:T(512)S(1)} %get-tuple-element.7, f32[512]{0:T(512)S(1)} %fusion.10), channel_id=1, replica_groups=mesh['batch'=16,'proto'=16] {'proto'}, use_global_device_ids=true, to_apply=%region_3.4 | all-reduce | flops 1024 | bytes 8192 | tf_op jit(solution)/shard_map/psum | solution.py:67
  379.5 9.5 %multiply_reduce_fusion = (f32[]{:T(128)}, bf16[512,4096]{1,0:T(8,128)(2,1)S(1)}) fusion(f32[512,4096]{1,0:T(8,128)} %get-tuple-element.8, f32[512]{0:T(512)S(1)} %log.3, f32[512,4096]{1,0:T(8,128)} %get-tuple-element.10, f32[512]{0:T(512)S(1)} %get-tuple-element.4, f32[4096]{0:T(1024)S(1)} %psum.82, f32[512]{0:T(512)S(1)} %psum.81, f32[4096]{0:T(1024)S(1)} %psum.80, ...), kind=kLoop, calls=%fused_computation.9 | loop fusion | flops 27262976 | bytes 21028868 | tf_op jit(solution)/shard_map/reduce_sum | solution.py:69
  389.0 2.0 copy-done
  390.9 2.1 fusion.27
  393.1 5.4 fusion.26
  399.2 77.3 %psum.87 = f32[]{:T(128)} all-reduce(f32[]{:T(128)S(6)} %neg.3), channel_id=1, replica_groups=mesh['batch'=16,'proto'=16] {'batch','proto'}, use_global_device_ids=true, to_apply=%region_24.25 | all-reduce | flops 1 | bytes 8 | tf_op jit(solution)/shard_map/psum | solution.py:70
  477.9 21.5 %psum.86 = f32[512]{0:T(512)S(1)} all-reduce(f32[512]{0:T(512)S(1)} %fusion.22), channel_id=1, replica_groups=mesh['batch'=16,'proto'=16] {'proto'}, use_global_device_ids=true, to_apply=%region_22.23 | all-reduce | flops 512 | bytes 4096 | tf_op jit(solution)/shard_map/psum | solution.py:93
  500.8 63.2 %all-reduce.3.cloned.1.call-done = f32[256,4096]{1,0:T(8,128)} async-done(((f32[256,4096]{1,0:T(8,128)}), f32[256,4096]{1,0:T(8,128)}) %all-reduce.3.cloned.1.call-update) | async-done | bytes 4194320 | tf_op jit(solution)/shard_map/psum | solution.py:81
  565.0 72.4 %psum.85 = f32[4096]{0:T(1024)S(1)} all-reduce(f32[4096]{0:T(1024)S(1)} %fusion.17), channel_id=1, replica_groups=mesh['batch'=16,'proto'=16] {'batch'}, use_global_device_ids=true, to_apply=%region_19.20 | all-reduce | flops 4096 | bytes 32768 | tf_op jit(solution)/shard_map/psum | solution.py:92
  (59 shorter events, 15.6 us)
Async XLA Ops:
  7.2 55.8 %all-gather.2.cloned.1.call-start = ((), (), s32[]{:S(2)}) async-start(), calls=%async_computation.1 | async-start | bytes 2228224 | tf_op jit(solution)/shard_map/all_gather | solution.py:50
  7.9 469.2 %reduce-scatter.2.cloned.1.call-start = ((), (), s32[]{:S(2)}) async-start(), calls=%async_computation.3 | async-start | bytes 557056 | tf_op jit(solution)/shard_map/reduce_scatter | solution.py:84
  7.9 21.5 %collective-permute-start.1 = (bf16[16,512]{1,0:T(8,128)(2,1)}, bf16[16,512]{1,0:T(8,128)(2,1)S(1)}, u32[]{:S(2)}, u32[]{:S(2)}) collective-permute-start(bf16[16,512]{1,0:T(8,128)(2,1)} %param.3), channel_id=1, source_target_pairs={{0,15},{1,0},{2,1},{3,2},{4,3},{5,4},{6,5},{7,6},{8,7},{9,8},{10,9... | collective-permute-start | bytes 49160 | tf_op jit(solution)/shard_map/ppermute | solution.py:26
  8.0 22.4 %collective-permute-start = (bf16[16,512]{1,0:T(8,128)(2,1)}, bf16[16,512]{1,0:T(8,128)(2,1)S(1)}, u32[]{:S(2)}, u32[]{:S(2)}) collective-permute-start(bf16[16,512]{1,0:T(8,128)(2,1)} %param.3), channel_id=1, source_target_pairs={{0,1},{1,2},{2,3},{3,4},{4,5},{5,6},{6,7},{7,8},{8,9},{9,10},{10,1... | collective-permute-start | bytes 49160 | tf_op jit(solution)/shard_map/ppermute | solution.py:21
  29.4 2.4 collective-permute-start.3
  30.3 3.6 collective-permute-start.2
  31.8 3.6 collective-permute-start.5
  33.9 3.6 collective-permute-start.4
  35.4 3.6 collective-permute-start.7
  37.5 3.2 collective-permute-start.6
  38.9 3.2 collective-permute-start.9
  40.6 3.5 collective-permute-start.8
  42.1 3.5 collective-permute-start.11
  44.1 3.4 collective-permute-start.10
  45.5 6.3 collective-permute-start.13
  47.5 4.4 collective-permute-start.12
  51.9 3.6 collective-permute-start.14
  388.9 2.0 copy-start
  393.1 171.0 %all-reduce.3.cloned.1.call-start = ((), (), s32[]{:S(2)}) async-start(), calls=%async_computation.2 | async-start | bytes 8388608 | tf_op jit(solution)/shard_map/psum | solution.py:81
Sparse Core Ops, SparseCore 0:
  10.4 52.5 all-gather.1
  393.2 51.1 reduce-scatter.1
  448.1 115.8 all-reduce.2
